TPU v7x, 512 devices: a whole 4x4x16 slice. The times are simulated.
512 devices in a mesh: gx: 8 (over x, z_hi), gy: 8 (over y, core), gz: 8 (over z_lo).
Axes of the slice: x: 4, y: 4, z: 16 (z_hi: 2, z_lo: 8; z = z_hi * 8 + z_lo), core: 2. Of those that a mesh axis runs over, the one named last changes fastest.
Arguments:
- positions: float32 [8, 8, 16, 3, 128], P('gx', 'gy', 'gz'), may hold values from 0 to 16, as said below
- block_fill: int32 [8, 8, 16], P('gx', 'gy', 'gz'), may hold values from 16 to 128, as said below
- noise: float32 [8, 8, 16, 8, 384], P('gx', 'gy', 'gz'), may hold values from -6 to 6
- pair_list: int32 [8, 8, 8, 3, 54], P('gx', 'gy', 'gz'), may hold values from 0 to 26, as said below
- pair_count: int32 [8, 8, 8], P('gx', 'gy', 'gz'), may hold values from 2 to 54, as said below
Outputs:
- displacement: float32 [8, 8, 16, 8, 384], P('gx', 'gy', 'gz')
Inputs may be any that keep to these rules, and one draw needn't show every extreme that they name: `positions`: each bead of cell (x, y, z) lies in the unit cube with corner (x, y, z). `block_fill`: beads of a block occupy its first slots. `pair_list`: in each device's list, the first pair_count slots hold field 0, a block index below 2; field 1, a neighbour code 9 (dx + 1) + 3 (dy + 1) + (dz + 1) with dx, dy, dz in -1..1 whose cell lies inside the grid; field 2, the owner flag. The relation is symmetric: a pair is listed on the first block's device exactly when the reverse pair is listed on the second block's device, and exactly one of the two carries owner flag 1; every block lists itself with code 13 and flag 1. Later slots hold 0, 13, 0. `pair_count`: counts the listed pairs of the device, each block's own pair included; some device lists every neighbour inside the grid of each of its blocks.
All inputs are finite; a program needn't handle non-finite values.
Results may differ from a plain program's by a relative error of at most 0.0025.
Values may be sent and summed in bfloat16 or wider, within the bound.
A program may use at most 64 MiB of HBM per device.

v0:
```python
import jax
import jax.numpy as jnp
from jax import lax
from jax.sharding import PartitionSpec as P

ITERS = 3
ROOT_ITERS = 12


radius = 0.08
floor_sq = 0.0001
epsilon = 1e-06
group_pairs = 8


def padded_2(array, sides, width):
    for axis, dim in sides:
        count, length = (lax.axis_size(axis), array.shape[dim])
        up = [(i, (i + 1) % count) for i in range(count - 1)]
        down = [(j, i) for i, j in up]
        last = lax.slice_in_dim(array, length - width, length, axis=dim)
        leading = lax.slice_in_dim(array, 0, width, axis=dim)
        before = lax.ppermute(last, axis, up)
        after = lax.ppermute(leading, axis, down)
        array = jnp.concatenate([before, array, after], axis=dim)
    return array


def mobility_tiles(first_pos, second_pos):
    offset = second_pos[:, :, None, :] - first_pos[:, :, :, None]
    dist_sq = (
        offset[:, 0] * offset[:, 0] + offset[:, 1] * offset[:, 1] + offset[:, 2] * offset[:, 2]
    )
    inverse_sq = 1.0 / jnp.maximum(dist_sq, floor_sq)
    distance = jnp.sqrt(dist_sq)
    reach_ratio = radius * jnp.sqrt(inverse_sq)
    far_iso = 0.75 * reach_ratio * (1.0 + 2.0 / 3.0 * radius * radius * inverse_sq)
    far_dyad = 0.75 * reach_ratio * (1.0 - 2.0 * radius * radius * inverse_sq)
    near_iso = 1.0 - 9.0 / 32.0 * distance / radius
    near_dyad = 3.0 / 32.0 * distance / radius
    apart = dist_sq >= 4.0 * radius * radius
    isotropic = jnp.where(apart, far_iso, near_iso)
    dyadic = jnp.where(apart, far_dyad, near_dyad) * inverse_sq
    identity_three = jnp.eye(3, dtype=jnp.float32)
    offset_t = jnp.transpose(offset, (0, 2, 1, 3))
    product = offset[:, :, :, None, :] * offset_t[:, None, :, :, :]
    mobility = (
        identity_three[None, :, None, :, None] * isotropic[:, None, :, None, :]
        + dyadic[:, None, :, None, :] * product
    )
    group_size = first_pos.shape[0]
    bead_count = first_pos.shape[2]
    return mobility.reshape(group_size, 3 * bead_count, 3 * bead_count).astype(jnp.bfloat16)


def inverse_three(matrix):
    cofactor = [
        [
            matrix[(line_index + 1) % 3][(place_index + 1) % 3]
            * matrix[(line_index + 2) % 3][(place_index + 2) % 3]
            - matrix[(line_index + 1) % 3][(place_index + 2) % 3]
            * matrix[(line_index + 2) % 3][(place_index + 1) % 3]
            for place_index in range(3)
        ]
        for line_index in range(3)
    ]
    determinant = (
        matrix[0][0] * cofactor[0][0]
        + matrix[0][1] * cofactor[0][1]
        + matrix[0][2] * cofactor[0][2]
    )
    return [
        [cofactor[place_index][line_index] / determinant for place_index in range(3)]
        for line_index in range(3)
    ]


def root_first_column(diagonal, coupling):
    zero_entry = jnp.zeros_like(diagonal[0])
    one_entry = jnp.ones_like(diagonal[0])
    trace_scale = (diagonal[0] + diagonal[1] + diagonal[2]) / 3.0
    tridiagonal = [
        [diagonal[0], coupling[0], zero_entry],
        [coupling[0], diagonal[1], coupling[1]],
        [zero_entry, coupling[1], diagonal[2]],
    ]
    root_guess = [
        [matrix_entry / trace_scale for matrix_entry in matrix_line] for matrix_line in tridiagonal
    ]
    partner = [
        [one_entry if line_index == place_index else zero_entry for place_index in range(3)]
        for line_index in range(3)
    ]
    for repeat_index in range(ROOT_ITERS):
        inverse_partner = inverse_three(partner)
        inverse_guess = inverse_three(root_guess)
        root_guess, partner = (
            [
                [
                    0.5
                    * (
                        root_guess[line_index][place_index]
                        + inverse_partner[line_index][place_index]
                    )
                    for place_index in range(3)
                ]
                for line_index in range(3)
            ],
            [
                [
                    0.5
                    * (partner[line_index][place_index] + inverse_guess[line_index][place_index])
                    for place_index in range(3)
                ]
                for line_index in range(3)
            ],
        )
    root_scale = jnp.sqrt(trace_scale)
    return [root_scale * root_guess[line_index][0] for line_index in range(3)]


def local_dot(left, right):
    return jnp.sum(left * right, axis=(0, 1, 2, 4))


def neighbour_index(block_ids, neighbour_codes, padded_depth):
    return (
        (neighbour_codes // 9 * 3 + neighbour_codes // 3 % 3) * padded_depth
        + block_ids
        + neighbour_codes % 3
    )


def body(positions, block_fill, noise, pair_list, pair_count):
    blocks = positions.shape[2]
    bead_count = positions.shape[4]
    samples = noise.shape[3]
    row_width = 3 * bead_count
    padded_depth = blocks + 2
    padded_cells = 9 * padded_depth
    capacity = pair_list.shape[4]
    bead_slots = lax.broadcasted_iota(jnp.int32, (1, 1, blocks, bead_count), 3)
    live_mask = jnp.tile((bead_slots < block_fill[..., None]).astype(jnp.float32), (1, 1, 1, 3))[
        :, :, :, None, :
    ]
    padded_pos = padded_2(positions, (("gx", 0), ("gy", 1), ("gz", 2)), 1).reshape(
        padded_cells, 3, bead_count
    )
    block_ids = pair_list[0, 0, 0, 0]
    neighbour_codes = pair_list[0, 0, 0, 1]
    pair_total = pair_count[0, 0, 0]
    home_index = 4 * padded_depth + 1 + block_ids
    away_index = neighbour_index(block_ids, neighbour_codes, padded_depth)
    group_turns = (pair_total + group_pairs - 1) // group_pairs

    def select_group(group_index):
        slot_index = group_index * group_pairs + lax.iota(jnp.int32, group_pairs)
        valid_mask = (slot_index < pair_total).astype(jnp.float32)
        return (jnp.minimum(slot_index, capacity - 1), valid_mask)

    start_vec = noise * live_mask
    start_norm = jnp.sqrt(lax.psum(local_dot(start_vec, start_vec), ("gx", "gy", "gz")) + epsilon)
    current = start_vec / start_norm[:, None]
    previous = jnp.zeros_like(current)
    beta_prev = jnp.zeros((samples,), jnp.float32)
    basis = []
    diagonal = []
    coupling = []
    for repeat_index in range(ITERS):
        basis.append(current)
        padded = padded_2(
            current.astype(jnp.bfloat16), (("gx", 0), ("gy", 1), ("gz", 2)), 1
        ).reshape(padded_cells, samples, row_width)

        def accumulate(group_index, running):
            slot_index, valid_mask = select_group(group_index)
            home_pick = home_index[slot_index]
            away_pick = away_index[slot_index]
            mobility = mobility_tiles(padded_pos[home_pick], padded_pos[away_pick])
            contribution = jnp.einsum(
                "gsk,gmk->gsm", padded[away_pick], mobility, preferred_element_type=jnp.float32
            )
            return running.at[block_ids[slot_index]].add(contribution * valid_mask[:, None, None])

        running = lax.fori_loop(
            0, group_turns, accumulate, jnp.zeros((blocks, samples, row_width), jnp.float32)
        )
        image_vec = running.reshape(1, 1, blocks, samples, row_width) * live_mask
        alpha_now = lax.psum(local_dot(current, image_vec), ("gx", "gy", "gz"))
        diagonal.append(alpha_now)
        if repeat_index + 1 < ITERS:
            residual = image_vec - alpha_now[:, None] * current - beta_prev[:, None] * previous
            beta_now = jnp.sqrt(
                lax.psum(local_dot(residual, residual), ("gx", "gy", "gz")) + epsilon
            )
            coupling.append(beta_now)
            previous = current
            current = residual / beta_now[:, None]
            beta_prev = beta_now
    weights = root_first_column(diagonal, coupling)
    result = (start_norm * weights[0])[:, None] * basis[0]
    for repeat_index in range(1, ITERS):
        result = result + (start_norm * weights[repeat_index])[:, None] * basis[repeat_index]
    return result


def solution(mesh):
    in_specs = (
        P("gx", "gy", "gz", None, None),
        P("gx", "gy", "gz"),
        P("gx", "gy", "gz", None, None),
        P("gx", "gy", "gz", None, None),
        P("gx", "gy", "gz"),
    )
    out_specs = P("gx", "gy", "gz", None, None)
    return jax.shard_map(body, mesh=mesh, in_specs=in_specs, out_specs=out_specs, check_vma=False)
```

profile of v0, /device:TPU:1, one launch (start us, length us, event | category | flops | bytes accessed | tf_op | source)
XLA Modules:
  0.0 1561.3 jit_solution(2802343237340308095)
XLA Ops:
  1.6 111.0 %psum.42 = f32[8]{0:T(128)S(1)} all-reduce(f32[8]{0:T(128)S(1)} %multiply_reduce_fusion.2), channel_id=1, replica_groups=mesh['gx'=8,'gy'=8,'gz'=8] {'gx','gy','gz'}, use_global_device_ids=true, to_apply=%region_1.2 | all-reduce | flops 8 | bytes 64 | tf_op jit(solution)/shard_map/psum | solution.py:162
  113.5 7.1 collective-permute-start
  121.9 12.7 collective-permute-start.6
  138.6 9.2 collective-permute-done.7
  173.7 153.3 %while.36 = (s32[]{:T(128)}, f32[2,8,384]{2,1,0:T(8,128)S(1)}, s32[]{:T(128)}, s32[54]{0:T(128)S(1)}, s32[54]{0:T(128)S(1)}, /*index=5*/bf16[36,8,384]{2,1,0:T(8...) while((s32[]{:T(128)}, f32[2,8,384]{2,1,0:T(8,128)S(1)}, ...), condition=%wide.region_4.5_spmd, body=%wide.region_2.4_spmd.sunk | while | flops 28363932 | bytes 50746348 | solution.py:185
  178.9 4.6 multiply_multiply_fusion.9
  183.5 8.5 mul.4877
  196.0 8.5 mul.4879
  206.0 4.6 fusion.106
  217.3 4.6 multiply_multiply_fusion.9
  221.8 8.5 mul.4877
  234.3 8.5 mul.4879
  244.3 4.6 fusion.106
  255.6 4.6 multiply_multiply_fusion.9
  260.1 8.5 mul.4877
  272.7 8.5 mul.4879
  282.7 4.6 fusion.106
  293.9 4.6 multiply_multiply_fusion.9
  298.5 8.5 mul.4877
  311.0 8.5 mul.4879
  321.0 4.6 fusion.106
  327.3 216.3 %psum.43 = f32[8]{0:T(128)S(1)} all-reduce(f32[8]{0:T(128)S(1)} %fusion.57), channel_id=1, replica_groups=mesh['gx'=8,'gy'=8,'gz'=8] {'gx','gy','gz'}, use_global_device_ids=true, to_apply=%region_6.7 | all-reduce | flops 8 | bytes 64 | tf_op jit(solution)/shard_map/psum | solution.py:189
  543.8 98.3 %psum.44 = f32[8]{0:T(128)S(1)} all-reduce(f32[8]{0:T(128)S(1)} %multiply_reduce_fusion.1), channel_id=1, replica_groups=mesh['gx'=8,'gy'=8,'gz'=8] {'gx','gy','gz'}, use_global_device_ids=true, to_apply=%region_8.9 | all-reduce | flops 8 | bytes 64 | tf_op jit(solution)/shard_map/psum | solution.py:194
  643.4 5.9 collective-permute-start.12
  650.6 11.9 collective-permute-done.13
  662.5 4.9 collective-permute-start.14
  680.6 153.5 %while.37 = (s32[]{:T(128)}, f32[2,8,384]{2,1,0:T(8,128)S(1)}, s32[]{:T(128)}, s32[54]{0:T(128)S(1)}, s32[54]{0:T(128)S(1)}, /*index=5*/bf16[36,8,384]{2,1,0:T(8...) while((s32[]{:T(128)}, f32[2,8,384]{2,1,0:T(8,128)S(1)}, ...), condition=%wide.region_11.12_spmd, body=%wide.region_9.11_spmd.sunk | while | flops 28363932 | bytes 50746348 | solution.py:185
  685.9 4.6 multiply_multiply_fusion.10
  690.5 8.5 mul.4898
  703.0 8.5 mul.4900
  713.0 4.6 fusion.113
  724.3 4.6 multiply_multiply_fusion.10
  728.8 8.5 mul.4898
  741.3 8.5 mul.4900
  751.3 4.6 fusion.113
  762.6 4.6 multiply_multiply_fusion.10
  767.1 8.5 mul.4898
  779.7 8.5 mul.4900
  789.7 4.6 fusion.113
  800.9 4.6 multiply_multiply_fusion.10
  805.5 8.5 mul.4898
  818.0 8.5 mul.4900
  828.0 4.6 fusion.113
  834.9 215.1 %psum.45 = f32[8]{0:T(128)S(1)} all-reduce(f32[8]{0:T(128)S(1)} %fusion.55), channel_id=1, replica_groups=mesh['gx'=8,'gy'=8,'gz'=8] {'gx','gy','gz'}, use_global_device_ids=true, to_apply=%region_13.14 | all-reduce | flops 8 | bytes 64 | tf_op jit(solution)/shard_map/psum | solution.py:189
  1051.0 98.7 %psum.46 = f32[8]{0:T(128)S(1)} all-reduce(f32[8]{0:T(128)S(1)} %get-tuple-element.551), channel_id=1, replica_groups=mesh['gx'=8,'gy'=8,'gz'=8] {'gx','gy','gz'}, use_global_device_ids=true, to_apply=%region_15.16 | all-reduce | flops 8 | bytes 64 | tf_op jit(solution)/shard_map/psum | solution.py:194
  1149.8 6.9 collective-permute-start.18
  1158.0 11.9 collective-permute-done.19
  1169.9 4.6 collective-permute-start.20
  1186.6 153.6 %while.38 = (s32[]{:T(128)}, f32[2,8,384]{2,1,0:T(8,128)S(1)}, s32[]{:T(128)}, s32[54]{0:T(128)S(1)}, s32[54]{0:T(128)S(1)}, /*index=5*/bf16[36,8,384]{2,1,0:T(8...) while((s32[]{:T(128)}, f32[2,8,384]{2,1,0:T(8,128)S(1)}, ...), condition=%wide.region_18.19_spmd, body=%wide.region_16.18_spmd.sunk | while | flops 28363932 | bytes 50746348 | solution.py:185
  1192.0 4.6 multiply_multiply_fusion.11
  1196.5 8.5 mul.4919
  1209.1 8.5 mul.4921
  1219.1 4.6 fusion.120
  1230.3 4.6 multiply_multiply_fusion.11
  1234.9 8.5 mul.4919
  1247.4 8.5 mul.4921
  1257.4 4.6 fusion.120
  1273.2 8.5 mul.4919
  1285.8 8.5 mul.4921
  1295.7 4.6 fusion.120
  1311.5 8.5 mul.4919
  1324.1 8.5 mul.4921
  1334.1 4.6 fusion.120
  1341.1 216.3 %psum.47 = f32[8]{0:T(128)S(1)} all-reduce(f32[8]{0:T(128)S(1)} %fusion.54), channel_id=1, replica_groups=mesh['gx'=8,'gy'=8,'gz'=8] {'gx','gy','gz'}, use_global_device_ids=true, to_apply=%region_20.21 | all-reduce | flops 8 | bytes 64 | tf_op jit(solution)/shard_map/psum | solution.py:189
  (388 shorter events, 222.4 us)
Async XLA Ops:
  112.6 9.2 copy-start.5
  113.5 40.5 %collective-permute-start = (bf16[1,1,2,8,384]{4,3,2,1,0:T(8,128)(2,1)S(1)}, bf16[1,1,2,8,384]{4,3,2,1,0:T(8,128)(2,1)S(1)}, u32[]{:S(2)}, u32[]{:S(2)}) collective-permute-start(bf16[1,1,2,8,384]{4,3,2,1,0:T(8,128)(2,1)S(1)} %fusion.66), channel_id=1, source_target_pairs={{0,64},{64,128},{128,192},{192,256},{256,320},{320,384},{384,448},... | collective-permute-start | bytes 36872 | tf_op jit(solution)/shard_map/ppermute | solution.py:23
  120.6 33.3 %collective-permute-start.1 = (bf16[1,1,2,8,384]{4,3,2,1,0:T(8,128)(2,1)S(1)}, bf16[1,1,2,8,384]{4,3,2,1,0:T(8,128)(2,1)S(1)}, u32[]{:S(2)}, u32[]{:S(2)}) collective-permute-start(bf16[1,1,2,8,384]{4,3,2,1,0:T(8,128)(2,1)S(1)} %fusion.66), channel_id=1, source_target_pairs={{64,0},{128,64},{192,128},{256,192},{320,256},{384,320},{448,384},... | collective-permute-start | bytes 36872 | tf_op jit(solution)/shard_map/ppermute | solution.py:24
  121.9 16.0 %collective-permute-start.6 = (f32[1,1,2,3,128]{4,2,3,1,0:T(2,128)}, f32[1,1,2,3,128]{4,2,3,1,0:T(2,128)S(1)}, u32[]{:S(2)}, u32[]{:S(2)}) collective-permute-start(f32[1,1,2,3,128]{4,2,3,1,0:T(2,128)} %param.11), channel_id=1, source_target_pairs={{0,64},{64,128},{128,192},{192,256},{256,320},{320,384},{384,448},... | collective-permute-start | bytes 9224 | tf_op jit(solution)/shard_map/ppermute | solution.py:23
  134.6 13.3 collective-permute-start.7
  147.9 11.3 collective-permute-start.8
  151.7 7.6 collective-permute-start.9
  153.9 10.3 collective-permute-start.2
  157.3 7.0 collective-permute-start.3
  159.3 10.4 collective-permute-start.10
  163.0 6.7 collective-permute-start.11
  164.3 5.4 collective-permute-start.4
  168.3 5.3 collective-permute-start.5
  173.7 153.4 %copy-start = (f32[1,1,2,8,384]{4,3,2,1,0:T(8,128)S(1)}, f32[1,1,2,8,384]{4,3,2,1,0:T(8,128)}, u32[]{:S(2)}) copy-start(f32[1,1,2,8,384]{4,3,2,1,0:T(8,128)} %param.13) | copy-start | bytes 73732
  543.6 137.0 %copy-start.2 = (f32[8]{0:T(128)}, f32[8]{0:T(128)S(1)}, u32[]{:S(2)}) copy-start(f32[8]{0:T(128)S(1)} %psum.43) | copy-start | bytes 100
  642.1 0.6 copy-start.7
  643.4 7.2 collective-permute-start.12
  649.3 13.2 collective-permute-start.13
  662.5 6.9 collective-permute-start.14
  667.4 5.3 collective-permute-start.15
  672.7 4.2 collective-permute-start.16
  675.6 4.9 collective-permute-start.17
  1050.0 0.9 copy-start.6
  1050.9 135.6 %copy-start.1 = (f32[1,1,2,8,384]{4,3,2,1,0:T(8,128)}, f32[1,1,2,8,384]{4,3,2,1,0:T(8,128)S(1)}, u32[]{:S(2)}) copy-start(f32[1,1,2,8,384]{4,3,2,1,0:T(8,128)S(1)} %get-tuple-element.552) | copy-start | bytes 73732
  1149.7 36.9 %copy-start.8 = (f32[8]{0:T(128)}, f32[8]{0:T(128)S(1)}, u32[]{:S(2)}) copy-start(f32[8]{0:T(128)S(1)} %psum.46) | copy-start | bytes 100
  1149.7 36.9 %copy-start.4 = (f32[8]{0:T(128)}, f32[8]{0:T(128)S(1)}, u32[]{:S(2)}) copy-start(f32[8]{0:T(128)S(1)} %add_sqrt_fusion) | copy-start | bytes 100
  1149.8 8.2 collective-permute-start.18
  1156.7 13.2 collective-permute-start.19
  1169.9 6.5 collective-permute-start.20
  1174.5 5.3 collective-permute-start.21
  1179.9 3.0 collective-permute-start.22
  1181.6 4.9 collective-permute-start.23
  1186.5 370.8 %copy-start.3 = (f32[8]{0:T(128)S(1)}, f32[8]{0:T(128)}, u32[]{:S(2)}) copy-start(f32[8]{0:T(128)} %copy-done.2) | copy-start | bytes 100
where the time goes:
time: 1570 us; the launch traced here: 1560 us
  blocking collectives  956 us (61%)
  local copies, waits for them, and re-layouts  304 us (19%)
  other arithmetic  113 us (7%)
  starting transfers between devices  79.8 us (5%)
  matrix products  54.9 us (3%)
  waiting for transfers between devices  50.8 us (3%)
    psum x3, blocking collectives, body(): alpha_now = lax.psum(local_dot(current, image_vec), ('gx', 'gy', 'gz'))  648 us
    psum x2, blocking collectives, body(): lax.psum(local_dot(residual, residual), ('gx', 'gy', 'gz')) + epsilon  197 us
    mul x36, local copies, waits for them, and re-layouts, mobility_tiles(): identity_three[None, :, None, :, None] * isotropic[:, None, :, None, :]  152 us
    psum x1, blocking collectives, body(): lax.psum(local_dot(start_vec, start_vec), ('gx', 'gy', 'gz')) + epsilon  111 us
    mul x12, local copies, waits for them, and re-layouts, mobility_tiles(): dyadic[:, None, :, None, :] * product  102 us
    ppermute x12, starting transfers between devices, padded_2(): before = lax.ppermute(last, axis, up)  61.4 us
    dot_general x12, matrix products, accumulate(): jnp.einsum('gsk,gmk->gsm', padded[away_pick], mobility, preferred_element...  54.9 us
    mul x12, other arithmetic, mobility_tiles(): dyadic[:, None, :, None, :] * product  54.6 us
  transfers between devices with their start and end apart: 24, of which 8 were waited for; matrix products, arithmetic and copies ran while one was open for 0% of the time, Pallas kernels for 0%

commit v1 on v0

v1 whole, which is shorter than its diff:
```python
import jax
import jax.numpy as jnp
from jax import lax
from jax.experimental import pallas as pl
from jax.experimental.pallas import tpu as pltpu
from jax.sharding import PartitionSpec as P

ROOT_ITERS = 12
RADIUS = 0.08
EPSILON = 1e-6
MESH = pl.DeviceIdType.MESH
BEAD = 128
SAMPLES = 8
CELL = 3 * SAMPLES
LEFT, MID, RIGHT = (0, 32), (32, 48), (80, 32)
PAIRS = ((0, 0), (0, 1), (1, 1), (0, 2), (1, 2), (1, 3))
f32, bf16 = jnp.float32, jnp.bfloat16


def tile_factors(d0, d1, d2):
    dist = d0 * d0 + d1 * d1 + d2 * d2
    root = lax.rsqrt(jnp.maximum(dist, 1e-30))
    capped = jnp.minimum(root, 100.0)
    inv = capped * capped
    length = dist * root
    far_iso = capped * (0.75 * RADIUS + (0.5 * RADIUS**3) * inv)
    far_dyad = capped * (0.75 * RADIUS - (1.5 * RADIUS**3) * inv)
    near_iso = 1.0 - (9.0 / 32.0 / RADIUS) * length
    near_dyad = (3.0 / 32.0 / RADIUS) * length
    apart = dist >= 4.0 * RADIUS * RADIUS
    return jnp.where(apart, far_iso, near_iso), jnp.where(apart, far_dyad, near_dyad) * inv


def inverse_three(m):
    def cof(i, j):
        a, b, c, d = (i + 1) % 3, (i + 2) % 3, (j + 1) % 3, (j + 2) % 3
        return m[a][c] * m[b][d] - m[a][d] * m[b][c]

    co = [[cof(i, j) for j in range(3)] for i in range(3)]
    scale = 1.0 / (m[0][0] * co[0][0] + m[0][1] * co[0][1] + m[0][2] * co[0][2])
    return [[co[j][i] * scale for j in range(3)] for i in range(3)]


def combination(moments):
    def inner(left, right):
        total = 0.0
        for i, a in enumerate(left):
            for j, b in enumerate(right):
                total = total + a * b * moments[i + j]
        return total

    def apply(v):
        return [v[0]] + [v[i] + v[i - 1] for i in range(1, len(v))] + [v[-1]]

    norm = jnp.sqrt(moments[0] + EPSILON)
    v1 = [1.0 / norm]
    w1 = apply(v1)
    a1 = inner(v1, w1)
    r1 = [w1[0] - a1 * v1[0], w1[1]]
    b1 = jnp.sqrt(inner(r1, r1) + EPSILON)
    v2 = [r / b1 for r in r1]
    w2 = apply(v2)
    a2 = inner(v2, w2)
    r2 = [w2[0] - a2 * v2[0] - b1 * v1[0], w2[1] - a2 * v2[1], w2[2]]
    b2 = jnp.sqrt(inner(r2, r2) + EPSILON)
    v3 = [r / b2 for r in r2]
    a3 = inner(v3, apply(v3))
    scale = (a1 + a2 + a3) / 3.0
    zero, one = jnp.zeros_like(a1), jnp.ones_like(a1)
    y = [[e / scale for e in row] for row in ((a1, b1, zero), (b1, a2, b2), (zero, b2, a3))]
    z = [[one if i == j else zero for j in range(3)] for i in range(3)]

    def step(_, state):
        y, z = state
        iz, iy = inverse_three(z), inverse_three(y)
        return (
            [[0.5 * (y[i][j] + iz[i][j]) for j in range(3)] for i in range(3)],
            [[0.5 * (z[i][j] + iy[i][j]) for j in range(3)] for i in range(3)],
        )

    y, z = lax.fori_loop(0, ROOT_ITERS, step, (y, z))
    root = [jnp.sqrt(scale) * y[i][0] for i in range(3)]
    return [
        norm * (root[0] * v1[0] + root[1] * v2[0] + root[2] * v3[0]),
        norm * (root[1] * v2[1] + root[2] * v3[1]),
        norm * (root[2] * v3[2]),
    ]


def kernel(
    fill_ref, count_ref, list_ref, pos_ref, noise_ref, out_ref,
    meta_src, start_src, pos_halo, start_own, halo, own, back, tiles, columns, weights,
    sums_z, sums_xy, row_buf,
    move_send, move_recv, back_send, back_recv, pos_send, pos_recv, u_send, u_recv,
    z_send, z_recv, xy_send, xy_recv,
):
    ix, iy, iz = lax.axis_index("gx"), lax.axis_index("gy"), lax.axis_index("gz")
    nx = lax.axis_size("gx") // 2
    ny = lax.axis_size("gy")
    half = lax.axis_size("gz")
    nz = 2 * half
    my_x, my_z = lax.div(ix, 2), lax.rem(ix, 2) * half + iz

    def device(x, y, z):
        return (2 * x + lax.div(z, half), y, lax.rem(z, half))

    def shifted(dx, dy, dz):
        return device(
            lax.rem(my_x + dx + nx, nx), lax.rem(iy + dy + ny, ny), lax.rem(my_z + dz + nz, nz)
        )

    barrier = pltpu.get_barrier_semaphore()

    def greet(dx, dy, dz):
        pl.semaphore_signal(barrier, inc=1, device_id=shifted(dx, dy, dz), device_id_type=MESH)

    @pl.loop(1, nz)
    def _(k):
        greet(0, 0, k)

    @pl.loop(1, nx * ny)
    def _(k):
        greet(lax.div(k, ny), lax.rem(k, ny), 0)

    @pl.loop(0, 16)
    def _(k):
        q = lax.rem(k, 8)
        q = q + lax.div(q + 4, 8)
        greet(lax.div(q, 3) - 1, lax.rem(q, 3) - 1, 2 * lax.div(k, 8) - 1)

    lanes = lax.broadcasted_iota(jnp.int32, (1, BEAD), 1)
    slots = list_ref.shape[1]
    codes = lax.broadcasted_iota(jnp.int32, (BEAD, slots), 0)
    live = lax.broadcasted_iota(jnp.int32, (1, slots), 1) < count_ref[0]
    chosen = jnp.where(codes == list_ref[1:2, :], 1.0, 0.0).astype(bf16)
    masks = []
    for b in range(2):
        mask = jnp.where(lanes < fill_ref[b], 1.0, 0.0)
        masks.append(mask)
        here = jnp.where(live & (list_ref[0:1, :] == b), 1.0, 0.0)
        here = jnp.broadcast_to(here, (SAMPLES, slots)).astype(bf16)
        tally = lax.dot_general(
            here, chosen, (((1,), (1,)), ((), ())), preferred_element_type=f32
        )
        meta_src[b, 0:3, :] = pos_ref[b]
        meta_src[b, 3:4, :] = mask
        meta_src[b, 4:5, :] = tally[0:1]
        meta_src[b, 5:8, :] = jnp.zeros((3, BEAD), f32)
        for c in range(3):
            start_src[b, c * 8 : c * 8 + 8, :] = noise_ref[b, :, c * BEAD : (c + 1) * BEAD] * mask

    pl.semaphore_wait(barrier, (nz - 1) + (nx * ny - 1) + 16)

    def move(src, dst, send, recv, target):
        tx, ty, tz = target
        same = (tx == ix) & (tz == iz)

        @pl.when(same)
        def _():
            pltpu.make_async_copy(src, dst, recv).start()

        @pl.when(jnp.logical_not(same))
        def _():
            pltpu.make_async_remote_copy(
                src, dst, send, recv, device_id=target, device_id_type=MESH
            ).start()

    def moved(src, send, target):
        tx, ty, tz = target
        same = (tx == ix) & (tz == iz)

        @pl.when(jnp.logical_not(same))
        def _():
            pltpu.make_async_remote_copy(
                src, src, send, send, device_id=target, device_id_type=MESH
            ).wait_send()

    def landed(dst, recv):
        pltpu.make_async_copy(dst, dst, recv).wait()

    side = lax.rem(ix, 2)
    for b in range(2):
        target = device(my_x, iy, 2 * iz + b)
        move(meta_src.at[b], pos_halo.at[4, 1 + side], move_send.at[0, b], move_recv.at[0, side], target)
    for b in range(2):
        target = device(my_x, iy, 2 * iz + b)
        move(start_src.at[b], start_own.at[side], move_send.at[1, b], move_recv.at[1, side], target)
    for h in range(2):
        landed(pos_halo.at[4, 1 + h], move_recv.at[0, h])

    def exchange(src_of, dst_of, send, recv):
        def copy(dc, part, dx):
            dy, dz = 1 - lax.rem(dc, 3), 1 - lax.div(dc, 3)
            return pltpu.make_async_remote_copy(
                src_of(part), dst_of(dc, part), send.at[dc, part], recv.at[dc, part],
                device_id=shifted(dx, dy, dz), device_id_type=MESH,
            )

        return copy

    def start_column(copy, dc, middle):
        copy(dc, 0, 1).start()
        copy(dc, 2, -1).start()
        if middle:
            copy(dc, 1, 0).start()

    def sent_column(copy, dc, middle):
        copy(dc, 0, 1).wait_send()
        copy(dc, 2, -1).wait_send()
        if middle:
            copy(dc, 1, 0).wait_send()

    def arrived_column(copy, dc, middle):
        copy(dc, 0, 1).wait_recv()
        copy(dc, 2, -1).wait_recv()
        if middle:
            copy(dc, 1, 0).wait_recv()

    def column(t):
        return lax.rem(t + 4, 9)

    def exchange_start(copy, count):
        start_column(copy, 4, False)

        @pl.loop(1, count)
        def _(t):
            start_column(copy, column(t), True)

    def exchange_sent(copy, count):
        sent_column(copy, 4, False)

        @pl.loop(1, count)
        def _(t):
            sent_column(copy, column(t), True)

    pos_src = {0: (2, 1), 1: (1, 2), 2: (1, 1)}
    pos_dst = {0: (0, 1), 1: (1, 2), 2: (3, 1)}
    pos_copy = exchange(
        lambda part: pos_halo.at[4, pl.ds(*pos_src[part])],
        lambda dc, part: pos_halo.at[dc, pl.ds(*pos_dst[part])],
        pos_send, pos_recv,
    )
    exchange_start(pos_copy, 9)

    own_mask = []
    for h in range(2):
        own_mask.append(pos_halo[4, 1 + h, 3:4, :])
        table = jnp.transpose(pos_halo[4, 1 + h], (1, 0))
        weights[h] = jnp.broadcast_to(table[:, 4:5], (BEAD, BEAD))

    u_src = {0: (48, 32), 1: (32, 48), 2: (32, 32)}
    u_dst = {0: LEFT, 1: MID, 2: RIGHT}

    def u_copy(n):
        return exchange(
            lambda part: halo.at[n, 4, pl.ds(*u_src[part])],
            lambda dc, part: halo.at[n, dc, pl.ds(*u_dst[part])],
            u_send.at[n], u_recv.at[n],
        )

    copies = [u_copy(n) for n in range(3)]
    for h in range(2):
        landed(start_own.at[h], move_recv.at[1, h])
    start = jnp.concatenate([start_own[0], start_own[1]], axis=0)
    own[0] = start
    halo[0, 4, MID[0] : MID[0] + MID[1], :] = start.astype(bf16)
    exchange_start(copies[0], 9)

    def build(dc):
        for xs in range(4):
            columns[xs] = jnp.transpose(pos_halo[dc, xs], (1, 0))
        mine = [[pos_halo[4, 1 + a, c : c + 1, :] for c in range(3)] for a in range(2)]

        @pl.loop(0, BEAD // 16)
        def _(r):
            row = pl.multiple_of(r * 16, 16)
            away = []
            for xs in range(4):
                block = columns[xs, pl.ds(row, 16), :]
                away.append(
                    [jnp.broadcast_to(block[:, c : c + 1], (16, BEAD)) for c in range(3)]
                )
            for q, (a, xs) in enumerate(PAIRS):
                d = [away[xs][c] - mine[a][c] for c in range(3)]
                iso, dyad = tile_factors(*d)
                scaled = [dyad * d[c] for c in range(3)]
                for c in range(3):
                    for e in range(c, 3):
                        entry = scaled[c] * d[e]
                        entry = (entry + iso if c == e else entry).astype(bf16)
                        for e2, c2 in {(e, c), (c, e)}:
                            tiles[
                                dc * 6 + q, pl.ds(e2 * BEAD + row, 16), c2 * BEAD : (c2 + 1) * BEAD
                            ] = entry

    arrived_column(pos_copy, 4, False)
    build(4)

    @pl.loop(1, 9)
    def _(t):
        dc = column(t)
        arrived_column(pos_copy, dc, True)
        build(dc)

    def column_products(n, dc, picks):
        u = halo[n, dc].astype(f32)
        outs = [None, None]
        for q in picks:
            a, xs = PAIRS[q]
            code = 9 * (xs - a) + 3 * lax.rem(dc, 3) + lax.div(dc, 3)
            weight = weights[a, pl.ds(code, 1), :]
            rows = [u[8 + 24 * xs + 8 * e : 16 + 24 * xs + 8 * e] * weight for e in range(3)]
            term = jnp.dot(
                jnp.concatenate(rows, axis=1).astype(bf16), tiles[dc * 6 + q],
                preferred_element_type=f32,
            )
            outs[a] = term if outs[a] is None else outs[a] + term
        return outs

    def matvec(n, count):
        arrived_column(copies[n], 4, False)
        if count == 9:
            first = column_products(n, 4, range(6))
        else:
            first = column_products(n, 4, (3, 5))

        def step(t, acc):
            dc = column(t)
            arrived_column(copies[n], dc, True)
            outs = column_products(n, dc, range(6))
            return acc[0] + outs[0], acc[1] + outs[1]

        acc = lax.fori_loop(1, count, step, (first[0], first[1]))
        if count < 9:
            home = column_products(n, 4, (1, 4))
            acc = (2.0 * acc[0] + home[0], 2.0 * acc[1] + home[1])
        rows = []
        for a in range(2):
            for c in range(3):
                rows.append(acc[a][:, c * BEAD : (c + 1) * BEAD] * own_mask[a])
        full = jnp.concatenate(rows, axis=0)
        return full - halo[n, 4, MID[0] : MID[0] + MID[1], :].astype(f32)

    def fold(left, right):
        product = left * right
        total = product[0:8]
        for k in range(1, 6):
            total = total + product[8 * k : 8 * k + 8]
        return total

    def homeward(h):
        return (2 * my_x + h, iy, lax.div(my_z, 2))

    current = own[0]
    parts = [fold(current, current)]
    for n in range(2):
        nxt = matvec(n, 9)
        own[n + 1] = nxt
        halo[n + 1, 4, MID[0] : MID[0] + MID[1], :] = nxt.astype(bf16)
        exchange_start(copies[n + 1], 9 if n == 0 else 5)
        for h in range(2):
            move(
                own.at[n + 1, pl.ds(h * CELL, CELL)], back.at[n, lax.rem(my_z, 2)],
                back_send.at[n, h], back_recv.at[n, lax.rem(my_z, 2)], homeward(h),
            )
        parts += [fold(current, nxt), fold(nxt, nxt)]
        current = nxt
    parts.append(fold(current, matvec(2, 5)))

    ones = jnp.ones((SAMPLES, BEAD), f32)
    row = lax.dot_general(
        ones, jnp.concatenate(parts + [jnp.zeros((BEAD - 48, BEAD), f32)], axis=0),
        (((1,), (1,)), ((), ())), precision=lax.Precision.HIGHEST, preferred_element_type=f32,
    )

    def z_copy(k):
        return pltpu.make_async_remote_copy(
            sums_z.at[pl.ds(0, 1)], sums_z.at[pl.ds(k, 1)], z_send.at[k], z_recv.at[k],
            device_id=shifted(0, 0, k), device_id_type=MESH,
        )

    def xy_copy(k):
        return pltpu.make_async_remote_copy(
            sums_xy.at[pl.ds(0, 1)], sums_xy.at[pl.ds(k, 1)], xy_send.at[k], xy_recv.at[k],
            device_id=shifted(lax.div(k, ny), lax.rem(k, ny), 0), device_id_type=MESH,
        )

    def all_sum(buffer, copy, count, value):
        buffer[0:1, :] = value

        @pl.loop(1, count)
        def _(k):
            copy(k).start()

        @pl.loop(1, count)
        def _(k):
            copy(k).wait_recv()

        total = jnp.sum(buffer[...], axis=0, keepdims=True)

        @pl.loop(1, count)
        def _(k):
            copy(k).wait_send()

        return total

    total = all_sum(sums_z, z_copy, nz, row[0:1])
    total = all_sum(sums_xy, xy_copy, nx * ny, total)
    total = jnp.broadcast_to(total, (SAMPLES, BEAD))
    moments = [total] + [pltpu.roll(total, BEAD - 8 * m, 1) for m in range(1, 6)]
    mix = combination(moments)
    for m in range(3):
        row_buf[m : m + 1, :] = mix[m][0:1]
    row_buf[3:8, :] = jnp.zeros((5, BEAD), f32)
    mixed = jnp.transpose(row_buf[...], (1, 0))[0:SAMPLES]

    for n in range(2):
        for b in range(2):
            landed(back.at[n, b], back_recv.at[n, b])
    for b in range(2):
        for c in range(3):
            rows = slice(c * 8, c * 8 + 8)
            out_ref[b, :, c * BEAD : (c + 1) * BEAD] = (
                mixed[:, 0:1] * start_src[b, rows, :]
                + mixed[:, 1:2] * back[0, b, rows, :]
                + mixed[:, 2:3] * back[1, b, rows, :]
            )

    for b in range(2):
        target = device(my_x, iy, 2 * iz + b)
        moved(meta_src.at[b], move_send.at[0, b], target)
        moved(start_src.at[b], move_send.at[1, b], target)
    for n in range(2):
        for h in range(2):
            moved(own.at[n + 1, pl.ds(h * CELL, CELL)], back_send.at[n, h], homeward(h))
    exchange_sent(pos_copy, 9)
    exchange_sent(copies[0], 9)
    exchange_sent(copies[1], 9)
    exchange_sent(copies[2], 5)


def body(positions, block_fill, noise, pair_list, pair_count):
    nx, ny, nz = lax.axis_size("gx") // 2, lax.axis_size("gy"), 2 * lax.axis_size("gz")
    dma = pltpu.SemaphoreType.DMA
    vmem, smem = pl.BlockSpec(memory_space=pltpu.VMEM), pl.BlockSpec(memory_space=pltpu.SMEM)
    out = pl.pallas_call(
        kernel,
        out_shape=jax.ShapeDtypeStruct((2, SAMPLES, 3 * BEAD), f32),
        in_specs=[smem, smem, vmem, vmem, vmem],
        out_specs=vmem,
        scratch_shapes=[
            pltpu.VMEM((2, 8, BEAD), f32),
            pltpu.VMEM((2, CELL, BEAD), f32),
            pltpu.VMEM((9, 4, 8, BEAD), f32),
            pltpu.VMEM((2, CELL, BEAD), f32),
            pltpu.VMEM((3, 9, 112, BEAD), bf16),
            pltpu.VMEM((3, 2 * CELL, BEAD), f32),
            pltpu.VMEM((2, 2, CELL, BEAD), f32),
            pltpu.VMEM((54, 3 * BEAD, 3 * BEAD), bf16),
            pltpu.VMEM((4, BEAD, 8), f32),
            pltpu.VMEM((2, BEAD, BEAD), f32),
            pltpu.VMEM((nz, BEAD), f32),
            pltpu.VMEM((nx * ny, BEAD), f32),
            pltpu.VMEM((8, BEAD), f32),
            dma((2, 2)), dma((2, 2)), dma((2, 2)), dma((2, 2)),
            dma((9, 3)), dma((9, 3)), dma((3, 9, 3)), dma((3, 9, 3)),
            dma((nz,)), dma((nz,)), dma((nx * ny,)), dma((nx * ny,)),
        ],
        compiler_params=pltpu.CompilerParams(
            collective_id=0, has_side_effects=True, vmem_limit_bytes=40 * 1024 * 1024
        ),
    )(
        block_fill.reshape(2), pair_count.reshape(1), pair_list.reshape(3, -1),
        positions.reshape(2, 3, BEAD), noise.reshape(2, SAMPLES, 3 * BEAD),
    )
    return out.reshape(noise.shape)


def solution(mesh):
    cells = P("gx", "gy", "gz", None, None)
    in_specs = (cells, P("gx", "gy", "gz"), cells, cells, P("gx", "gy", "gz"))
    return jax.shard_map(body, mesh=mesh, in_specs=in_specs, out_specs=cells, check_vma=False)
```

time: 1570 us -> 75.8 us (0.05)
  blocking collectives: 956 us -> 0 us
  local copies, waits for them, and re-layouts: 304 us -> 3.36 us
  other arithmetic: 113 us -> 0 us
  starting transfers between devices: 79.8 us -> 0 us
  Pallas kernels: 0 us -> 71.5 us
  matrix products: 54.9 us -> 0 us
  waiting for transfers between devices: 50.8 us -> 0 us
    psum x6 -> x0, blocking collectives: 956 us -> none  [the longest x3 648 us: body(): alpha_now = lax.psum(local_dot(current, image_vec), ('gx', 'gy', 'gz'))]
    mul x48 -> x0, local copies, waits for them, and re-layouts: 255 us -> none  [the longest x36 152 us: mobility_tiles(): identity_three[None, :, None, :, None] * isotropic[:, None, :, None, :]]
    ppermute x24 -> x0, starting transfers between devices: 79.8 us -> none  [the longest x12 61.4 us: padded_2(): before = lax.ppermute(last, axis, up)]
    pallas_call x0 -> x1, Pallas kernels: none -> 71.5 us  [body(): pl.pallas_call(kernel, out_shape=jax.ShapeDtypeStruct((2, SAMPLES, 3 * BE...]
    mul x14 -> x0, other arithmetic: 55.9 us -> none  [the longest x12 54.6 us: mobility_tiles(): dyadic[:, None, :, None, :] * product]
    dot_general x12 -> x0, matrix products: 54.9 us -> none  [accumulate(): jnp.einsum('gsk,gmk->gsm', padded[away_pick], mobility, preferred_element...]
    ppermute x24 -> x0, waiting for transfers between devices: 50.8 us -> none  [the longest x12 50.8 us: padded_2(): after = lax.ppermute(leading, axis, down)]
    gather x72 -> x0, local copies, waits for them, and re-layouts: 43.8 us -> none  [the longest x24 13.8 us: accumulate(): mobility = mobility_tiles(padded_pos[home_pick], padded_pos[away_pick])]
  transfers between devices with their start and end apart: 24 -> 0, of which waited for: 8 -> 0; matrix products, arithmetic and copies ran while one was open for 0% -> 0% of each run, Pallas kernels for 0% -> 0%
where the time goes in v1:
time: 75.8 us; the launch traced here: 75.5 us
  Pallas kernels  71.5 us (94%)
  local copies, waits for them, and re-layouts  3.36 us (4%)
    pallas_call x1, Pallas kernels, body(): pl.pallas_call(kernel, out_shape=jax.ShapeDtypeStruct((2, SAMPLES, 3 * BE...  71.5 us
    unnamed x11, local copies, waits for them, and re-layouts  3.36 us

profile of v1, /device:TPU:1, one launch (start us, length us, event | category | flops | bytes accessed | tf_op | source)
XLA Modules:
  0.0 75.5 jit_solution(13129032781202340567)
XLA Ops:
  0.7 0.0 copy-start.3
  0.7 0.7 copy-done.3
  1.3 0.0 copy-start.2
  1.3 0.7 copy-done.2
  2.0 0.0 copy-start.1
  2.0 0.7 copy-done.1
  2.7 0.0 copy-start
  2.7 0.7 copy-done
  3.4 71.5 %shard_map.55 = f32[2,8,384]{2,1,0:T(8,128)S(1)} custom-call(s32[2]{0:T(128)S(1)} %bitcast.15, s32[1]{0:T(128)} %bitcast.10.count_ref, s32[3,54]{1,0:T(4,128)S(1)} %bitcast.14, f32[2,3,128]{2,1,0:T(4,128)S(1)} %bitcast.13, f32[2,8,384]{2,1,0:T(8,128)S(1)} %bitcast.12), custom_call_target="tpu_custom_call" | custom-call | tf_op jit(solution)/shard_map/pallas_call | solution.py:446
  74.9 0.6 copy.14
  (2 shorter events, 0.0 us)
Async XLA Ops:
  0.7 0.7 copy-start.3
  1.3 0.7 copy-start.2
  2.0 0.7 copy-start.1
  2.7 0.7 copy-start

commit v2 on v1

v2 whole, which is shorter than its diff:
```python
import jax
import jax.numpy as jnp
from jax import lax
from jax.experimental import pallas as pl
from jax.experimental.pallas import tpu as pltpu
from jax.sharding import PartitionSpec as P

ROOT_ITERS = 12
RADIUS = 0.08
EPSILON = 1e-6
MESH = pl.DeviceIdType.MESH
BEAD = 128
SAMPLES = 8
CELL = 3 * SAMPLES
LEFT, MID, RIGHT = (0, 32), (32, 48), (80, 32)
PAIRS = ((0, 0), (0, 1), (0, 2), (1, 1), (1, 2), (1, 3))
WIDTH = 3 * BEAD
BLOCKS = ((0, 0), (0, 1), (0, 2), (1, 1), (1, 2), (2, 2))
NEAR_FIRST = (3, 5, 1, 7, 0, 2, 6, 8)
HALF_NEAR = (5, 7, 6, 8)
f32, bf16 = jnp.float32, jnp.bfloat16


def packed(order):
    return sum(dc * 9**t for t, dc in enumerate(order))


def each_column(order, body, carry=0):
    def step(_, state):
        digits, inside = state
        return lax.div(digits, 9), body(lax.rem(digits, 9), inside)

    return lax.fori_loop(0, len(order), step, (jnp.int32(packed(order)), carry))[1]


def tile_factors(d0, d1, d2):
    dist = d0 * d0 + d1 * d1 + d2 * d2
    root = lax.rsqrt(jnp.maximum(dist, 1e-30))
    capped = jnp.minimum(root, 100.0)
    inv = capped * capped
    length = dist * root
    far_iso = capped * (0.75 * RADIUS + (0.5 * RADIUS**3) * inv)
    far_dyad = capped * (0.75 * RADIUS - (1.5 * RADIUS**3) * inv)
    near_iso = 1.0 - (9.0 / 32.0 / RADIUS) * length
    near_dyad = (3.0 / 32.0 / RADIUS) * length
    apart = dist >= 4.0 * RADIUS * RADIUS
    return jnp.where(apart, far_iso, near_iso), jnp.where(apart, far_dyad, near_dyad) * inv


def inverse_three(m):
    def cof(i, j):
        a, b, c, d = (i + 1) % 3, (i + 2) % 3, (j + 1) % 3, (j + 2) % 3
        return m[a][c] * m[b][d] - m[a][d] * m[b][c]

    co = [[cof(i, j) for j in range(3)] for i in range(3)]
    scale = 1.0 / (m[0][0] * co[0][0] + m[0][1] * co[0][1] + m[0][2] * co[0][2])
    return [[co[j][i] * scale for j in range(3)] for i in range(3)]


def combination(moments):
    def inner(left, right):
        total = 0.0
        for i, a in enumerate(left):
            for j, b in enumerate(right):
                total = total + a * b * moments[i + j]
        return total

    def apply(v):
        return [v[0]] + [v[i] + v[i - 1] for i in range(1, len(v))] + [v[-1]]

    norm = jnp.sqrt(moments[0] + EPSILON)
    v1 = [1.0 / norm]
    w1 = apply(v1)
    a1 = inner(v1, w1)
    r1 = [w1[0] - a1 * v1[0], w1[1]]
    b1 = jnp.sqrt(inner(r1, r1) + EPSILON)
    v2 = [r / b1 for r in r1]
    w2 = apply(v2)
    a2 = inner(v2, w2)
    r2 = [w2[0] - a2 * v2[0] - b1 * v1[0], w2[1] - a2 * v2[1], w2[2]]
    b2 = jnp.sqrt(inner(r2, r2) + EPSILON)
    v3 = [r / b2 for r in r2]
    a3 = inner(v3, apply(v3))
    scale = (a1 + a2 + a3) / 3.0
    zero, one = jnp.zeros_like(a1), jnp.ones_like(a1)
    y = [[e / scale for e in row] for row in ((a1, b1, zero), (b1, a2, b2), (zero, b2, a3))]
    z = [[one if i == j else zero for j in range(3)] for i in range(3)]

    def step(_, state):
        y, z = state
        iz, iy = inverse_three(z), inverse_three(y)
        return (
            [[0.5 * (y[i][j] + iz[i][j]) for j in range(3)] for i in range(3)],
            [[0.5 * (z[i][j] + iy[i][j]) for j in range(3)] for i in range(3)],
        )

    y, z = lax.fori_loop(0, ROOT_ITERS, step, (y, z))
    root = [jnp.sqrt(scale) * y[i][0] for i in range(3)]
    return [
        norm * (root[0] * v1[0] + root[1] * v2[0] + root[2] * v3[0]),
        norm * (root[1] * v2[1] + root[2] * v3[1]),
        norm * (root[2] * v3[2]),
    ]


def kernel(
    fill_hbm, count_hbm, list_hbm, pos_hbm, noise_hbm, out_ref,
    fill_ref, count_ref, list_ref, pos_ref, noise_ref, meta_src, start_src, pos_halo, start_own, halo, own, back, tiles, columns, weights,
    sums_z, sums_xy, row_buf,
    input_sem, move_send, move_recv, back_send, back_recv, pos_send, pos_recv, u_send, u_recv,
    z_send, z_recv, xy_send, xy_recv,
):
    ix, iy, iz = lax.axis_index("gx"), lax.axis_index("gy"), lax.axis_index("gz")
    nx = lax.axis_size("gx") // 2
    ny = lax.axis_size("gy")
    half = lax.axis_size("gz")
    nz = 2 * half
    my_x, my_z = lax.div(ix, 2), lax.rem(ix, 2) * half + iz

    def device(x, y, z):
        return (2 * x + lax.div(z, half), y, lax.rem(z, half))

    def shifted(dx, dy, dz):
        return device(
            lax.rem(my_x + dx + nx, nx), lax.rem(iy + dy + ny, ny), lax.rem(my_z + dz + nz, nz)
        )

    inputs = [
        pltpu.make_async_copy(src, dst, input_sem.at[k])
        for k, (src, dst) in enumerate(
            (
                (fill_hbm, fill_ref), (count_hbm, count_ref), (list_hbm, list_ref),
                (pos_hbm, pos_ref), (noise_hbm, noise_ref),
            )
        )
    ]
    for copy in inputs:
        copy.start()

    barrier = pltpu.get_barrier_semaphore()

    def greet(dx, dy, dz):
        pl.semaphore_signal(barrier, inc=1, device_id=shifted(dx, dy, dz), device_id_type=MESH)

    @pl.loop(1, nz)
    def _(k):
        greet(0, 0, k)

    @pl.loop(1, nx * ny)
    def _(k):
        greet(lax.div(k, ny), lax.rem(k, ny), 0)

    @pl.loop(0, 16)
    def _(k):
        q = lax.rem(k, 8)
        q = q + lax.div(q + 4, 8)
        greet(lax.div(q, 3) - 1, lax.rem(q, 3) - 1, 2 * lax.div(k, 8) - 1)

    lanes = lax.broadcasted_iota(jnp.int32, (1, BEAD), 1)
    slots = list_ref.shape[2]
    for copy in inputs:
        copy.wait()
    codes = lax.broadcasted_iota(jnp.int32, (BEAD, slots), 0)
    live = lax.broadcasted_iota(jnp.int32, (1, slots), 1) < count_ref[0:1, 0:1]
    chosen = jnp.where(codes == list_ref[1], 1.0, 0.0).astype(bf16)
    masks = []
    for b in range(2):
        mask = jnp.where(lanes < fill_ref[0:1, b : b + 1], 1.0, 0.0)
        masks.append(mask)
        here = jnp.where(live & (list_ref[0] == b), 1.0, 0.0)
        here = jnp.broadcast_to(here, (SAMPLES, slots)).astype(bf16)
        tally = lax.dot_general(
            here, chosen, (((1,), (1,)), ((), ())), preferred_element_type=f32
        )
        for c in range(3):
            meta_src[b, c : c + 1, :] = pos_ref[c, b : b + 1, :]
        meta_src[b, 3:4, :] = mask
        meta_src[b, 4:5, :] = tally[0:1]
        meta_src[b, 5:8, :] = jnp.zeros((3, BEAD), f32)
        for c in range(3):
            start_src[b, c * 8 : c * 8 + 8, :] = noise_ref[b, :, c * BEAD : (c + 1) * BEAD] * mask

    pl.semaphore_wait(barrier, (nz - 1) + (nx * ny - 1) + 16)

    def move(src, dst, send, recv, target):
        tx, ty, tz = target
        same = (tx == ix) & (tz == iz)

        @pl.when(same)
        def _():
            pltpu.make_async_copy(src, dst, recv).start()

        @pl.when(jnp.logical_not(same))
        def _():
            pltpu.make_async_remote_copy(
                src, dst, send, recv, device_id=target, device_id_type=MESH
            ).start()

    def moved(src, send, target):
        tx, ty, tz = target
        same = (tx == ix) & (tz == iz)

        @pl.when(jnp.logical_not(same))
        def _():
            pltpu.make_async_remote_copy(
                src, src, send, send, device_id=target, device_id_type=MESH
            ).wait_send()

    def landed(dst, recv):
        pltpu.make_async_copy(dst, dst, recv).wait()

    side = lax.rem(ix, 2)
    for b in range(2):
        target = device(my_x, iy, 2 * iz + b)
        move(meta_src.at[b], pos_halo.at[4, 1 + side], move_send.at[0, b], move_recv.at[0, side], target)
    for b in range(2):
        target = device(my_x, iy, 2 * iz + b)
        move(start_src.at[b], start_own.at[side], move_send.at[1, b], move_recv.at[1, side], target)
    for h in range(2):
        landed(pos_halo.at[4, 1 + h], move_recv.at[0, h])

    def exchange(src_of, dst_of, column_of, send, recv):
        def copy(dc, part, dx):
            side_sem = 1 if isinstance(dc, int) else 0
            dy, dz = 1 - lax.rem(dc, 3), 1 - lax.div(dc, 3)
            return pltpu.make_async_remote_copy(
                src_of(part), dst_of(dc, part), send.at[side_sem], recv.at[dc],
                device_id=shifted(dx, dy, dz), device_id_type=MESH,
            )

        def start(order):
            def step(dc, carry):
                copy(dc, 0, 1).start()
                copy(dc, 2, -1).start()
                copy(dc, 1, 0).start()
                return carry

            each_column(order, step)
            copy(4, 0, 1).start()
            copy(4, 2, -1).start()

        def sent(order):
            bytes_of = column_of(slice(0, len(order)))
            pltpu.make_async_copy(bytes_of, bytes_of, send.at[0]).wait()
            sides = dst_of(4, 3)
            pltpu.make_async_copy(sides, sides, send.at[1]).wait()

        def arrived(dc):
            if isinstance(dc, int) and dc == 4:
                sides = dst_of(4, 3)
                pltpu.make_async_copy(sides, sides, recv.at[4]).wait()
            else:
                whole = column_of(dc)
                pltpu.make_async_copy(whole, whole, recv.at[dc]).wait()

        return start, sent, arrived

    def columns_of(ref, dc):
        return ref.at[pl.ds(0, dc.stop)] if isinstance(dc, slice) else ref.at[dc]

    pos_src = {0: (2, 1), 1: (1, 2), 2: (1, 1)}
    pos_dst = {0: (0, 1), 1: (1, 2), 2: (3, 1), 3: (0, 2)}
    pos_start, pos_sent, pos_arrived = exchange(
        lambda part: pos_halo.at[4, pl.ds(*pos_src[part])],
        lambda dc, part: pos_halo.at[dc, pl.ds(*pos_dst[part])],
        lambda dc: columns_of(pos_halo, dc), pos_send, pos_recv,
    )
    pos_start(NEAR_FIRST)

    own_mask = []
    for h in range(2):
        own_mask.append(pos_halo[4, 1 + h, 3:4, :])
        table = jnp.transpose(pos_halo[4, 1 + h], (1, 0))
        weights[h] = jnp.broadcast_to(table[:, 4:5], (BEAD, BEAD))

    u_src = {0: (48, 32), 1: (32, 48), 2: (32, 32)}
    u_dst = {0: LEFT, 1: MID, 2: RIGHT, 3: (0, 64)}

    def u_copy(n):
        return exchange(
            lambda part: halo.at[n, 4, pl.ds(*u_src[part])],
            lambda dc, part: halo.at[n, dc, pl.ds(*u_dst[part])],
            lambda dc: columns_of(halo.at[n], dc), u_send.at[n], u_recv.at[n],
        )

    copies = [u_copy(n) for n in range(3)]
    for h in range(2):
        landed(start_own.at[h], move_recv.at[1, h])
    start = jnp.concatenate([start_own[0], start_own[1]], axis=0)
    own[0] = start
    halo[0, 4, MID[0] : MID[0] + MID[1], :] = start.astype(bf16)
    copies[0][0](NEAR_FIRST)

    def build(dc):
        for xs in range(4):
            columns[xs] = jnp.transpose(pos_halo[dc, xs], (1, 0))
        mine = [[pos_halo[4, 1 + a, c : c + 1, :] for c in range(3)] for a in range(2)]

        @pl.loop(0, BEAD // 16, unroll=8)
        def _(r):
            row = pl.multiple_of(r * 16, 16)
            away = []
            for xs in range(4):
                block = columns[xs, pl.ds(row, 16), :]
                away.append(
                    [jnp.broadcast_to(block[:, c : c + 1], (16, BEAD)) for c in range(3)]
                )
            for q, (a, xs) in enumerate(PAIRS):
                d = [away[xs][c] - mine[a][c] for c in range(3)]
                iso, dyad = tile_factors(*d)
                scaled = [dyad * d[c] for c in range(3)]
                for k, (c, e) in enumerate(BLOCKS):
                    entry = scaled[c] * d[e]
                    entry = entry + iso if c == e else entry
                    tiles[dc, q, k, pl.ds(row, 16), :] = entry.astype(bf16)

    def products(n, a, dc, first, count):
        entries, blocks = [], []
        u = halo[n, dc].astype(f32)
        row, deep = (dc % 3, dc // 3) if isinstance(dc, int) else (lax.rem(dc, 3), lax.div(dc, 3))
        for xs in range(a + first, a + first + count):
            weight = weights[a, pl.ds(9 * (xs - a) + 3 * row + deep, 1), :]
            for e in range(3):
                entries.append(u[8 + 24 * xs + 8 * e : 16 + 24 * xs + 8 * e] * weight)
                parts = [
                    tiles[dc, 2 * a + xs, BLOCKS.index((min(c, e), max(c, e)))] for c in range(3)
                ]
                blocks.append(jnp.concatenate(parts, axis=1))
        return jnp.dot(
            jnp.concatenate(entries, axis=1).astype(bf16),
            jnp.concatenate(blocks, axis=0),
            preferred_element_type=f32,
        )

    pos_arrived(4)
    build(4)
    copies[0][2](4)

    def build_next(dc, state):
        before, left, right = state
        pos_arrived(dc)
        left = left + products(0, 0, before, 0, 3)
        right = right + products(0, 1, before, 0, 3)
        build(dc)
        copies[0][2](dc)
        return dc, left, right

    blank = jnp.zeros((SAMPLES, WIDTH), f32)
    state = each_column(NEAR_FIRST, build_next, (jnp.int32(4), blank, blank))
    image = [state[1 + a] + products(0, a, state[0], 0, 3) for a in range(2)]

    def matvec(n):
        arrived = copies[n][2]
        if n == 0:
            acc = image
        elif n == 1:
            acc = [0.0, 0.0]
            for dc in (4, *NEAR_FIRST):
                arrived(dc)
                acc = [acc[a] + products(n, a, dc, 0, 3) for a in range(2)]
        else:
            arrived(4)
            acc = [products(n, a, 4, 2, 1) for a in range(2)]
            for dc in HALF_NEAR:
                arrived(dc)
                acc = [acc[a] + products(n, a, dc, 0, 3) for a in range(2)]
            acc = [2.0 * acc[a] + products(n, a, 4, 1, 1) for a in range(2)]
        rows = []
        for a in range(2):
            for c in range(3):
                rows.append(acc[a][:, c * BEAD : (c + 1) * BEAD] * own_mask[a])
        full = jnp.concatenate(rows, axis=0)
        return full - halo[n, 4, MID[0] : MID[0] + MID[1], :].astype(f32)

    def fold(left, right):
        product = left * right
        total = product[0:8]
        for k in range(1, 6):
            total = total + product[8 * k : 8 * k + 8]
        return total

    def homeward(h):
        return (2 * my_x + h, iy, lax.div(my_z, 2))

    current = own[0]
    parts = [fold(current, current)]
    for n in range(2):
        nxt = matvec(n)
        own[n + 1] = nxt
        halo[n + 1, 4, MID[0] : MID[0] + MID[1], :] = nxt.astype(bf16)
        copies[n + 1][0](NEAR_FIRST if n == 0 else HALF_NEAR)
        for h in range(2):
            move(
                own.at[n + 1, pl.ds(h * CELL, CELL)], back.at[n, lax.rem(my_z, 2)],
                back_send.at[n, h], back_recv.at[n, lax.rem(my_z, 2)], homeward(h),
            )
        parts += [fold(current, nxt), fold(nxt, nxt)]
        current = nxt
        copies[n][1](NEAR_FIRST)
        if n == 0:
            pos_sent(NEAR_FIRST)
            for b in range(2):
                target = device(my_x, iy, 2 * iz + b)
                moved(meta_src.at[b], move_send.at[0, b], target)
                moved(start_src.at[b], move_send.at[1, b], target)
    parts.append(fold(current, matvec(2)))

    ones = jnp.ones((SAMPLES, BEAD), f32)
    row = lax.dot_general(
        ones, jnp.concatenate(parts + [jnp.zeros((BEAD - 48, BEAD), f32)], axis=0),
        (((1,), (1,)), ((), ())), precision=lax.Precision.HIGHEST, preferred_element_type=f32,
    )

    def all_sum(buffer, send, recv, count, shift, value, between):
        buffer[0:1, :] = value

        @pl.loop(1, count)
        def _(k):
            pltpu.make_async_remote_copy(
                buffer.at[pl.ds(0, 1)], buffer.at[pl.ds(k, 1)], send, recv,
                device_id=shift(k), device_id_type=MESH,
            ).start()

        between()
        others = buffer.at[pl.ds(1, count - 1)]
        pltpu.make_async_copy(others, others, recv).wait()
        return jnp.sum(buffer[...], axis=0, keepdims=True)

    def all_sent(buffer, send, count):
        others = buffer.at[pl.ds(1, count - 1)]
        pltpu.make_async_copy(others, others, send).wait()

    def tidy_halo():
        copies[2][1](HALF_NEAR)
        for n in range(2):
            for h in range(2):
                moved(own.at[n + 1, pl.ds(h * CELL, CELL)], back_send.at[n, h], homeward(h))

    def tidy_back():
        for n in range(2):
            for b in range(2):
                landed(back.at[n, b], back_recv.at[n, b])
        all_sent(sums_z, z_send, nz)

    total = all_sum(sums_z, z_send, z_recv, nz, lambda k: shifted(0, 0, k), row[0:1], tidy_halo)
    total = all_sum(
        sums_xy, xy_send, xy_recv, nx * ny,
        lambda k: shifted(lax.div(k, ny), lax.rem(k, ny), 0), total, tidy_back,
    )
    total = jnp.broadcast_to(total, (SAMPLES, BEAD))
    moments = [total] + [pltpu.roll(total, BEAD - 8 * m, 1) for m in range(1, 6)]
    mix = combination(moments)
    for m in range(3):
        row_buf[m : m + 1, :] = mix[m][0:1]
    row_buf[3:8, :] = jnp.zeros((5, BEAD), f32)
    mixed = jnp.transpose(row_buf[...], (1, 0))[0:SAMPLES]

    for b in range(2):
        for c in range(3):
            rows = slice(c * 8, c * 8 + 8)
            out_ref[b, :, c * BEAD : (c + 1) * BEAD] = (
                mixed[:, 0:1] * start_src[b, rows, :]
                + mixed[:, 1:2] * back[0, b, rows, :]
                + mixed[:, 2:3] * back[1, b, rows, :]
            )

    all_sent(sums_xy, xy_send, nx * ny)


def body(positions, block_fill, noise, pair_list, pair_count):
    nx, ny, nz = lax.axis_size("gx") // 2, lax.axis_size("gy"), 2 * lax.axis_size("gz")
    dma = pltpu.SemaphoreType.DMA
    vmem, hbm = pl.BlockSpec(memory_space=pltpu.VMEM), pl.BlockSpec(memory_space=pltpu.HBM)
    slots = pair_list.shape[-1]
    out = pl.pallas_call(
        kernel,
        out_shape=jax.ShapeDtypeStruct((2, SAMPLES, 3 * BEAD), f32),
        in_specs=[hbm] * 5,
        out_specs=vmem,
        scratch_shapes=[
            pltpu.VMEM((1, 2), jnp.int32),
            pltpu.VMEM((1, 1), jnp.int32),
            pltpu.VMEM((3, 1, slots), jnp.int32),
            pltpu.VMEM((3, 2, BEAD), f32),
            pltpu.VMEM((2, SAMPLES, WIDTH), f32),
            pltpu.VMEM((2, 8, BEAD), f32),
            pltpu.VMEM((2, CELL, BEAD), f32),
            pltpu.VMEM((9, 4, 8, BEAD), f32),
            pltpu.VMEM((2, CELL, BEAD), f32),
            pltpu.VMEM((3, 9, 112, BEAD), bf16),
            pltpu.VMEM((3, 2 * CELL, BEAD), f32),
            pltpu.VMEM((2, 2, CELL, BEAD), f32),
            pltpu.VMEM((9, 6, 6, BEAD, BEAD), bf16),
            pltpu.VMEM((4, BEAD, 8), f32),
            pltpu.VMEM((2, BEAD, BEAD), f32),
            pltpu.VMEM((nz, BEAD), f32),
            pltpu.VMEM((nx * ny, BEAD), f32),
            pltpu.VMEM((8, BEAD), f32),
            dma((5,)), dma((2, 2)), dma((2, 2)), dma((2, 2)), dma((2, 2)),
            dma((2,)), dma((9,)), dma((3, 2)), dma((3, 9)), dma, dma, dma, dma,
        ],
        compiler_params=pltpu.CompilerParams(
            collective_id=0, has_side_effects=True, vmem_limit_bytes=60 * 1024 * 1024
        ),
    )(
        block_fill.reshape(1, 2), pair_count.reshape(1, 1), pair_list.reshape(3, 1, slots),
        positions.reshape(2, 3, BEAD).transpose(1, 0, 2), noise.reshape(2, SAMPLES, 3 * BEAD),
    )
    return out.reshape(noise.shape)


def solution(mesh):
    cells = P("gx", "gy", "gz", None, None)
    in_specs = (cells, P("gx", "gy", "gz"), cells, cells, P("gx", "gy", "gz"))
    return jax.shard_map(body, mesh=mesh, in_specs=in_specs, out_specs=cells, check_vma=False)
```

time: 75.8 us -> 61.8 us (0.82)
  Pallas kernels: 71.5 us -> 59.6 us
  local copies, waits for them, and re-layouts: 3.36 us -> 1.35 us
    pallas_call x1, Pallas kernels: 71.5 us -> 59.6 us  [body(): pl.pallas_call(kernel, out_shape=jax.ShapeDtypeStruct((2, SAMPLES, 3 * BE...]
    unnamed x11 -> x1, local copies, waits for them, and re-layouts: 3.36 us -> 1.35 us
where the time goes in v2:
time: 61.8 us; the launch traced here: 61.6 us
  Pallas kernels  59.6 us (96%)
  local copies, waits for them, and re-layouts  1.35 us (2%)
  between operations  0.66 us (1%)
    pallas_call x1, Pallas kernels, body(): pl.pallas_call(kernel, out_shape=jax.ShapeDtypeStruct((2, SAMPLES, 3 * BE...  59.6 us
    unnamed x1, local copies, waits for them, and re-layouts  1.35 us

profile of v2, /device:TPU:1, one launch (start us, length us, event | category | flops | bytes accessed | tf_op | source)
XLA Modules:
  0.0 61.6 jit_solution(1390372772330588107)
XLA Ops:
  0.7 59.6 %shard_map.55 = f32[2,8,384]{2,1,0:T(8,128)} custom-call(s32[1,2]{1,0:T(1,128)} %bitcast.13, s32[1,1]{1,0:T(1,128)} %bitcast.8.count_hbm, s32[3,1,54]{2,1,0:T(1,128)} %bitcast.12, f32[3,2,128]{2,1,0:T(2,128)} %bitcast.11, f32[2,8,384]{2,1,0:T(8,128)} %bitcast.10), custom_call_target="tpu_custom_call" | custom-call | tf_op jit(solution)/shard_map/pallas_call | solution.py:475
  60.3 1.3 %copy.8 = f32[1,1,2,8,384]{4,3,2,1,0:T(8,128)} copy(f32[1,1,2,8,384]{4,3,2,1,0:T(8,128)} %bitcast.9) | data formatting | bytes 49152

commit v3 on v2

--- a/solution.py
+++ b/solution.py
@@ -115,10 +115,12 @@
     ny = lax.axis_size("gy")
     half = lax.axis_size("gz")
     nz = 2 * half
-    my_x, my_z = lax.div(ix, 2), lax.rem(ix, 2) * half + iz
+    turn = nz // 4
+    my_x, my_z = lax.div(ix, 2), lax.rem(lax.rem(ix, 2) * half + iz + turn, nz)
 
     def device(x, y, z):
-        return (2 * x + lax.div(z, half), y, lax.rem(z, half))
+        place = lax.rem(z + nz - turn, nz)
+        return (2 * x + lax.div(place, half), y, lax.rem(place, half))
 
     def shifted(dx, dy, dz):
         return device(
@@ -291,21 +293,20 @@
     halo[0, 4, MID[0] : MID[0] + MID[1], :] = start.astype(bf16)
     copies[0][0](NEAR_FIRST)
 
-    def build(dc):
-        for xs in range(4):
+    def build(dc, pairs=(0, 1, 2, 3, 4, 5)):
+        for xs in sorted({PAIRS[q][1] for q in pairs}):
             columns[xs] = jnp.transpose(pos_halo[dc, xs], (1, 0))
         mine = [[pos_halo[4, 1 + a, c : c + 1, :] for c in range(3)] for a in range(2)]
 
         @pl.loop(0, BEAD // 16, unroll=8)
         def _(r):
             row = pl.multiple_of(r * 16, 16)
-            away = []
-            for xs in range(4):
+            away = {}
+            for xs in sorted({PAIRS[q][1] for q in pairs}):
                 block = columns[xs, pl.ds(row, 16), :]
-                away.append(
-                    [jnp.broadcast_to(block[:, c : c + 1], (16, BEAD)) for c in range(3)]
-                )
-            for q, (a, xs) in enumerate(PAIRS):
+                away[xs] = [jnp.broadcast_to(block[:, c : c + 1], (16, BEAD)) for c in range(3)]
+            for q in pairs:
+                a, xs = PAIRS[q]
                 d = [away[xs][c] - mine[a][c] for c in range(3)]
                 iso, dyad = tile_factors(*d)
                 scaled = [dyad * d[c] for c in range(3)]
@@ -326,14 +327,17 @@
                     tiles[dc, 2 * a + xs, BLOCKS.index((min(c, e), max(c, e)))] for c in range(3)
                 ]
                 blocks.append(jnp.concatenate(parts, axis=1))
-        return jnp.dot(
-            jnp.concatenate(entries, axis=1).astype(bf16),
-            jnp.concatenate(blocks, axis=0),
-            preferred_element_type=f32,
-        )
-
+        total = None
+        for x in range(count):
+            left = jnp.concatenate(entries[3 * x : 3 * x + 3], axis=1).astype(bf16)
+            right = jnp.concatenate(blocks[3 * x : 3 * x + 3], axis=0)
+            term = jnp.dot(left, right, preferred_element_type=f32)
+            total = term if total is None else total + term
+        return total
+
+    build(4, (1, 2, 3, 4))
     pos_arrived(4)
-    build(4)
+    build(4, (0, 5))
     copies[0][2](4)
 
     def build_next(dc, state):
@@ -440,13 +444,13 @@
         for n in range(2):
             for b in range(2):
                 landed(back.at[n, b], back_recv.at[n, b])
-        all_sent(sums_z, z_send, nz)
-
-    total = all_sum(sums_z, z_send, z_recv, nz, lambda k: shifted(0, 0, k), row[0:1], tidy_halo)
+        all_sent(sums_xy, xy_send, nx * ny)
+
     total = all_sum(
         sums_xy, xy_send, xy_recv, nx * ny,
-        lambda k: shifted(lax.div(k, ny), lax.rem(k, ny), 0), total, tidy_back,
+        lambda k: shifted(lax.div(k, ny), lax.rem(k, ny), 0), row[0:1], tidy_halo,
     )
+    total = all_sum(sums_z, z_send, z_recv, nz, lambda k: shifted(0, 0, k), total, tidy_back)
     total = jnp.broadcast_to(total, (SAMPLES, BEAD))
     moments = [total] + [pltpu.roll(total, BEAD - 8 * m, 1) for m in range(1, 6)]
     mix = combination(moments)
@@ -464,7 +468,7 @@
                 + mixed[:, 2:3] * back[1, b, rows, :]
             )
 
-    all_sent(sums_xy, xy_send, nx * ny)
+    all_sent(sums_z, z_send, nz)
 
 
 def body(positions, block_fill, noise, pair_list, pair_count):

time: 61.8 us -> 61.1 us (0.989)
  Pallas kernels: 59.6 us -> 58.9 us
    pallas_call x1, Pallas kernels: 59.6 us -> 58.9 us  [body(): pl.pallas_call(kernel, out_shape=jax.ShapeDtypeStruct((2, SAMPLES, 3 * BE...]
where the time goes in v3:
time: 61.1 us; the launch traced here: 60.9 us
  Pallas kernels  58.9 us (96%)
  local copies, waits for them, and re-layouts  1.35 us (2%)
  between operations  0.66 us (1%)
    pallas_call x1, Pallas kernels, body(): pl.pallas_call(kernel, out_shape=jax.ShapeDtypeStruct((2, SAMPLES, 3 * BE...  58.9 us
    unnamed x1, local copies, waits for them, and re-layouts  1.35 us

profile of v3, /device:TPU:1, one launch (start us, length us, event | category | flops | bytes accessed | tf_op | source)
XLA Modules:
  0.0 60.9 jit_solution(11525308285213564462)
XLA Ops:
  0.7 58.9 %shard_map.55 = f32[2,8,384]{2,1,0:T(8,128)} custom-call(s32[1,2]{1,0:T(1,128)} %bitcast.13, s32[1,1]{1,0:T(1,128)} %bitcast.8.count_hbm, s32[3,1,54]{2,1,0:T(1,128)} %bitcast.12, f32[3,2,128]{2,1,0:T(2,128)} %bitcast.11, f32[2,8,384]{2,1,0:T(8,128)} %bitcast.10), custom_call_target="tpu_custom_call" | custom-call | tf_op jit(solution)/shard_map/pallas_call | solution.py:479
  59.6 1.3 %copy.8 = f32[1,1,2,8,384]{4,3,2,1,0:T(8,128)} copy(f32[1,1,2,8,384]{4,3,2,1,0:T(8,128)} %bitcast.9) | data formatting | bytes 49152

commit v4 on v3

--- a/solution.py
+++ b/solution.py
@@ -16,6 +16,7 @@
 PAIRS = ((0, 0), (0, 1), (0, 2), (1, 1), (1, 2), (1, 3))
 WIDTH = 3 * BEAD
 BLOCKS = ((0, 0), (0, 1), (0, 2), (1, 1), (1, 2), (2, 2))
+REACH = 5
 NEAR_FIRST = (3, 5, 1, 7, 0, 2, 6, 8)
 HALF_NEAR = (5, 7, 6, 8)
 f32, bf16 = jnp.float32, jnp.bfloat16
@@ -141,22 +142,27 @@
 
     barrier = pltpu.get_barrier_semaphore()
 
-    def greet(dx, dy, dz):
-        pl.semaphore_signal(barrier, inc=1, device_id=shifted(dx, dy, dz), device_id_type=MESH)
-
-    @pl.loop(1, nz)
+    def greet(target):
+        pl.semaphore_signal(barrier, inc=1, device_id=target, device_id_type=MESH)
+
+    def is_me(target):
+        return (target[0] == ix) & (target[2] == iz)
+
+    def greet_other(target):
+        @pl.when(jnp.logical_not(is_me(target)))
+        def _():
+            greet(target)
+
+    for h in range(2):
+        greet_other((2 * my_x + h, iy, lax.div(my_z, 2)))
+    for k in range(2, REACH + 1):
+        greet(shifted(0, 0, k))
+        greet(shifted(0, 0, -k))
+
+    @pl.loop(0, 26)
     def _(k):
-        greet(0, 0, k)
-
-    @pl.loop(1, nx * ny)
-    def _(k):
-        greet(lax.div(k, ny), lax.rem(k, ny), 0)
-
-    @pl.loop(0, 16)
-    def _(k):
-        q = lax.rem(k, 8)
-        q = q + lax.div(q + 4, 8)
-        greet(lax.div(q, 3) - 1, lax.rem(q, 3) - 1, 2 * lax.div(k, 8) - 1)
+        q = k + lax.div(k + 13, 26)
+        greet(shifted(lax.rem(lax.div(q, 3), 3) - 1, lax.rem(q, 3) - 1, lax.div(q, 9) - 1))
 
     lanes = lax.broadcasted_iota(jnp.int32, (1, BEAD), 1)
     slots = list_ref.shape[2]
@@ -182,7 +188,9 @@
         for c in range(3):
             start_src[b, c * 8 : c * 8 + 8, :] = noise_ref[b, :, c * BEAD : (c + 1) * BEAD] * mask
 
-    pl.semaphore_wait(barrier, (nz - 1) + (nx * ny - 1) + 16)
+    homes = [device(my_x, iy, 2 * iz + b) for b in range(2)]
+    stay = sum(jnp.where(is_me(target), 1, 0) for target in homes)
+    pl.semaphore_wait(barrier, 26 + 2 * (REACH - 1) + 2 - stay)
 
     def move(src, dst, send, recv, target):
         tx, ty, tz = target

time: 61.1 us -> 60.4 us (0.989)
  Pallas kernels: 58.9 us -> 58.2 us
    pallas_call x1, Pallas kernels: 58.9 us -> 58.2 us  [body(): pl.pallas_call(kernel, out_shape=jax.ShapeDtypeStruct((2, SAMPLES, 3 * BE...]
where the time goes in v4:
time: 60.4 us; the launch traced here: 60.2 us
  Pallas kernels  58.2 us (96%)
  local copies, waits for them, and re-layouts  1.35 us (2%)
  between operations  0.66 us (1%)
    pallas_call x1, Pallas kernels, body(): pl.pallas_call(kernel, out_shape=jax.ShapeDtypeStruct((2, SAMPLES, 3 * BE...  58.2 us
    unnamed x1, local copies, waits for them, and re-layouts  1.35 us

profile of v4, /device:TPU:1, one launch (start us, length us, event | category | flops | bytes accessed | tf_op | source)
XLA Modules:
  0.0 60.2 jit_solution(12150832916774084486)
XLA Ops:
  0.7 58.2 %shard_map.55 = f32[2,8,384]{2,1,0:T(8,128)} custom-call(s32[1,2]{1,0:T(1,128)} %bitcast.13, s32[1,1]{1,0:T(1,128)} %bitcast.8.count_hbm, s32[3,1,54]{2,1,0:T(1,128)} %bitcast.12, f32[3,2,128]{2,1,0:T(2,128)} %bitcast.11, f32[2,8,384]{2,1,0:T(8,128)} %bitcast.10), custom_call_target="tpu_custom_call" | custom-call | tf_op jit(solution)/shard_map/pallas_call | solution.py:487
  58.9 1.3 %copy.8 = f32[1,1,2,8,384]{4,3,2,1,0:T(8,128)} copy(f32[1,1,2,8,384]{4,3,2,1,0:T(8,128)} %bitcast.9) | data formatting | bytes 49152

commit v5 on v4

--- a/solution.py
+++ b/solution.py
@@ -268,12 +268,17 @@
     def columns_of(ref, dc):
         return ref.at[pl.ds(0, dc.stop)] if isinstance(dc, slice) else ref.at[dc]
 
+    def pos_rows(dc):
+        if isinstance(dc, slice):
+            return pos_halo.at[pl.ds(0, dc.stop), pl.ds(0, 4), pl.ds(0, 4)]
+        return pos_halo.at[dc, pl.ds(0, 4), pl.ds(0, 4)]
+
     pos_src = {0: (2, 1), 1: (1, 2), 2: (1, 1)}
     pos_dst = {0: (0, 1), 1: (1, 2), 2: (3, 1), 3: (0, 2)}
     pos_start, pos_sent, pos_arrived = exchange(
-        lambda part: pos_halo.at[4, pl.ds(*pos_src[part])],
-        lambda dc, part: pos_halo.at[dc, pl.ds(*pos_dst[part])],
-        lambda dc: columns_of(pos_halo, dc), pos_send, pos_recv,
+        lambda part: pos_halo.at[4, pl.ds(*pos_src[part]), pl.ds(0, 4)],
+        lambda dc, part: pos_halo.at[dc, pl.ds(*pos_dst[part]), pl.ds(0, 4)],
+        lambda dc: pos_rows(dc), pos_send, pos_recv,
     )
     pos_start(NEAR_FIRST)
 

time: 60.4 us -> 60.3 us (level)
  no operation moved by 1% of the time
where the time goes in v5:
time: 60.3 us; the launch traced here: 60.1 us
  Pallas kernels  58.1 us (96%)
  local copies, waits for them, and re-layouts  1.35 us (2%)
  between operations  0.66 us (1%)
    pallas_call x1, Pallas kernels, body(): pl.pallas_call(kernel, out_shape=jax.ShapeDtypeStruct((2, SAMPLES, 3 * BE...  58.1 us
    unnamed x1, local copies, waits for them, and re-layouts  1.35 us

profile of v5, /device:TPU:1, one launch (start us, length us, event | category | flops | bytes accessed | tf_op | source)
XLA Modules:
  0.0 60.1 jit_solution(3476619994952866763)
XLA Ops:
  0.7 58.1 %shard_map.55 = f32[2,8,384]{2,1,0:T(8,128)} custom-call(s32[1,2]{1,0:T(1,128)} %bitcast.13, s32[1,1]{1,0:T(1,128)} %bitcast.8.count_hbm, s32[3,1,54]{2,1,0:T(1,128)} %bitcast.12, f32[3,2,128]{2,1,0:T(2,128)} %bitcast.11, f32[2,8,384]{2,1,0:T(8,128)} %bitcast.10), custom_call_target="tpu_custom_call" | custom-call | tf_op jit(solution)/shard_map/pallas_call | solution.py:492
  58.8 1.3 %copy.8 = f32[1,1,2,8,384]{4,3,2,1,0:T(8,128)} copy(f32[1,1,2,8,384]{4,3,2,1,0:T(8,128)} %bitcast.9) | data formatting | bytes 49152
